TPU v7x, 32 devices: a whole 2x2x4 slice. The times are simulated.
32 devices in a mesh: feat: 8 (over y, x, core), node: 4 (over z).
Axes of the slice: x: 2, y: 2, z: 4, core: 2. Of those that a mesh axis runs over, the one named last changes fastest.
Arguments:
- features: bfloat16 [4, 512, 16384], P('node', 'feat'), may hold values from -6 to 6
- target_ids: int32 [4, 4096], P('node'), may hold values from 0 to 16383
- block_ids: int32 [4, 32, 8], P('node'), may hold values from 0 to 127
- tile_counts: int32 [4, 32], P('node'), may hold values from 1 to 8, as said below
- adjacency: bfloat16 [4, 32, 8, 128, 128], P('node'), may hold values from 0 to 0.25
- w_neigh: bfloat16 [256, 512], P(None, 'feat'), may hold values from -0.1875 to 0.1875
- w_self: bfloat16 [256, 512], P(None, 'feat'), may hold values from -0.1875 to 0.1875
- w_head: bfloat16 [256, 256], replicated, may hold values from -0.375 to 0.375
- grad_scores: bfloat16 [4, 4096, 256], P('node', 'feat'), may hold values from -6 to 6
Outputs:
- scores: bfloat16 [4, 4096, 256], P('node', 'feat')
- grad_head: float32 [256, 256], replicated
- grad_neigh: float32 [256, 512], P(None, 'feat')
- grad_self: float32 [256, 512], P(None, 'feat')
Inputs may be any that keep to these rules, and one draw needn't show every extreme that they name: `tile_counts`: one group, drawn from the seed, has all of its tiles at 8 live slots; every tile of the other groups has fewer than 8.
All inputs are finite; a program needn't handle non-finite values.
Results may differ from a plain program's by a relative error of at most 0.0056.
Values may be sent and summed in bfloat16 or wider, within the bound.
A program may use at most 64 MiB of HBM per device.

v0:
```python
import jax
import jax.numpy as jnp
from jax import lax
from jax.sharding import PartitionSpec as P


def aggregate_local(feature_rows, block_row, count_row, adjacency_group):
    width = feature_rows.shape[0]
    tiles = block_row.shape[0]
    slots = block_row.shape[1]
    blocks = feature_rows.reshape(width, -1, 128)
    gathered = jnp.take(blocks, block_row.reshape(-1), axis=1).reshape(width, tiles, slots, 128)
    live = (jnp.arange(slots, dtype=jnp.int32)[None, :] < count_row[:, None]).astype(jnp.bfloat16)
    masked = gathered * live[None, :, :, None]
    summed = jnp.einsum(
        "tkrs,ftks->ftr", adjacency_group, masked, preferred_element_type=jnp.float32
    )
    summed = summed / count_row.astype(jnp.float32)[None, :, None]
    return summed.astype(jnp.bfloat16).reshape(width, tiles * 128)


def contract_first(left, right):
    return lax.dot_general(
        left, right, (((0,), (1,)), ((), ())), preferred_element_type=jnp.float32
    )


def body(
    features, target_ids, block_ids, tile_counts, adjacency, w_neigh, w_self, w_head, grad_scores
):
    feature_rows = features[0]
    aggregate = aggregate_local(feature_rows, block_ids[0], tile_counts[0], adjacency[0])
    own = jnp.take(feature_rows, target_ids[0], axis=1)
    agg_part = aggregate
    own_part = own
    preact = lax.psum_scatter(
        contract_first(agg_part, w_neigh) + contract_first(own_part, w_self),
        "feat",
        scatter_dimension=0,
        tiled=True,
    )
    hidden = jax.nn.silu(preact).astype(jnp.bfloat16)
    scores = jnp.dot(hidden, w_head.T, preferred_element_type=jnp.float32).astype(jnp.bfloat16)
    cotangent = grad_scores[0]
    head_local = lax.dot_general(
        cotangent, hidden, (((0,), (0,)), ((), ())), preferred_element_type=jnp.float32
    )
    grad_head = lax.psum(head_local, ("feat", "node"))
    grad_hidden = jnp.dot(cotangent, w_head, preferred_element_type=jnp.float32)
    sigma = jax.nn.sigmoid(preact)
    grad_pre = (grad_hidden * sigma * (1.0 + preact * (1.0 - sigma))).astype(jnp.bfloat16)
    shard_piece = lax.all_gather(grad_pre, "feat", axis=0, tiled=True)
    agg_part = aggregate
    own_part = own
    neigh_local = contract_first(shard_piece, agg_part)
    self_local = contract_first(shard_piece, own_part)
    grad_neigh, grad_self = lax.psum((neigh_local, self_local), "node")
    return (scores[None], grad_head, grad_neigh, grad_self)


def solution(mesh):
    in_specs = (
        P("node", "feat", None),
        P("node", None),
        P("node", None, None),
        P("node", None),
        P("node", None, None, None, None),
        P(None, "feat"),
        P(None, "feat"),
        P(),
        P("node", "feat", None),
    )
    out_specs = (P("node", "feat", None), P(), P(None, "feat"), P(None, "feat"))
    return jax.shard_map(body, mesh=mesh, in_specs=in_specs, out_specs=out_specs, check_vma=False)
```

profile of v0, /device:TPU:0, one launch (start us, length us, event | category | flops | bytes accessed | tf_op | source)
XLA Modules:
  0.0 308.8 jit_solution(13335983999297234126)
XLA Ops:
  7.2 0.0 copy-start
  7.2 0.0 copy-start.1
  7.2 0.0 reduce-scatter.2.cloned.1.call-start
  7.2 0.8 compare_and_fusion.1
  8.1 0.8 copy.23
  8.8 0.7 bitcast_convert_fusion
  9.5 0.1 copy.22
  9.6 0.7 compare_select_fusion
  10.3 0.7 compare_and_fusion
  11.1 0.7 fusion.33
  11.8 0.1 reshape_squeeze.10
  11.9 4.8 %copy.26 = bf16[1,64,16384]{1,2,0:T(8,128)(2,1)} copy(bf16[1,64,16384]{2,1,0:T(8,128)(2,1)} %param.9) | data formatting | bytes 4194304 | tf_op args[0]
  16.7 0.0 copy-done.1
  16.7 0.6 copy.30
  17.3 1.4 copy.24
  18.6 3.1 gather_fusion
  21.7 0.0 copy-start.4
  21.7 13.8 %gather_fusion.1 = bf16[4096,64]{1,0:T(8,128)(2,1)S(1)} fusion(bf16[64,16384]{0,1:T(8,128)(2,1)} %bitcast.57, s32[4096]{0:T(1024)S(1)} %broadcast_clamp_fusion), kind=kCustom, calls=%fused_computation.1 | custom fusion | bytes 1064960 | tf_op jit(solution)/shard_map/jit(_take)/gather | solution.py:33
  35.5 0.0 copy-done.4
  35.5 0.0 copy-start.2
  35.5 1.5 fusion.29
  37.0 0.7 copy-done.2
  37.7 0.0 copy-start.5
  37.7 5.7 %fusion.19 = bf16[32,8,8,128]{3,2,1,0:T(8,128)(2,1)S(1)} fusion(bf16[1,32,8,128,128]{4,3,2,1,0:T(8,128)(2,1)} %param.13, bf16[64,32,8,128]{3,0,2,1:T(8,128)(2,1)S(1)} %bitcast.60, pred[32,8]{1,0:T(8,128)(4,1)S(1)} %copy.22, bf16[32,8]{1,0:T(8,128)(2,1)S(1)} %fusion.33, f32[32]{0:T(128)S(1)} %bitcast_convert_fusion), kind=kOutput, calls=%fused_computation.19 | convolution fusion | flops 541589504 | bytes 13108096 | tf_op jit(solution)/shard_map/tkrs,ftks->ftr/dot_general | solution.py:15
  43.4 0.0 copy-done.5
  43.4 2.7 convolution_add_fusion
  46.1 0.0 copy-start.7
  46.1 0.0 reduce-scatter.2.cloned.1.call-update
  46.1 0.0 all-gather.2.cloned.1.call-start
  46.2 54.1 %reduce-scatter.2.cloned.1.call-done = f32[512,256]{1,0:T(8,128)} async-done(((f32[4096,256]{1,0:T(8,128)}), f32[512,256]{1,0:T(8,128)}) %reduce-scatter.2.cloned.1.call-update) | async-done | bytes 524304 | tf_op jit(solution)/shard_map/reduce_scatter | solution.py:36
  100.3 0.0 copy-done
  100.3 0.0 copy-done.7
  100.3 2.0 fusion.13
  102.3 0.0 all-gather.2.cloned.1.call-update
  102.4 0.0 all-reduce.4.cloned.1.call-start
  102.4 2.1 convolution_bitcast_fusion
  104.5 0.0 copy-start.6
  104.5 0.0 all-reduce.4.cloned.1.call-update
  104.5 0.0 all-reduce.6.cloned.1.call-start
  104.6 26.3 %all-gather.2.cloned.1.call-done = bf16[4096,256]{1,0:T(8,128)(2,1)} async-done(((bf16[512,256]{1,0:T(8,128)(2,1)}), bf16[4096,256]{1,0:T(8,128)(2,1)}) %all-gather.2.cloned.1.call-update) | async-done | bytes 2097168 | tf_op jit(solution)/shard_map/all_gather | solution.py:52
  130.8 0.0 copy-start.3
  130.9 4.9 %fusion.30 = f32[256,64]{0,1:T(8,128)} fusion(bf16[4096,256]{1,0:T(8,128)(2,1)} %all-gather.2.cloned.1.call-done, bf16[4096,64]{1,0:T(8,128)(2,1)S(1)} %gather_fusion.1, pred[4096]{0:T(1024)(128)(4,1)S(1)} %compare_and_fusion), kind=kOutput, calls=%fused_computation.28 | convolution fusion | flops 134479872 | bytes 2691072 | tf_op jit(solution)/shard_map/dot_general | solution.py:23
  135.8 0.0 copy-done.3
  135.8 1.1 fusion.24
  136.9 0.0 all-reduce.6.cloned.1.call-update
  136.9 0.0 copy-done.6
  136.9 1.0 fusion.14
  137.9 124.9 %all-reduce.4.cloned.1.call-done = f32[256,256]{0,1:T(8,128)} async-done(((f32[256,256]{0,1:T(8,128)}), f32[256,256]{0,1:T(8,128)}) %all-reduce.4.cloned.1.call-update) | async-done | bytes 262160 | tf_op jit(solution)/shard_map/psum | solution.py:48
  262.9 1.8 copy.27
  264.6 34.7 %all-reduce.6.cloned.1.call-done = (f32[256,64]{0,1:T(8,128)}, f32[256,64]{0,1:T(8,128)}) async-done(((f32[256,64]{0,1:T(8,128)}, f32[256,64]{0,1:T(8,128)}), (f32[256,64]{0,1:T(8,128)}, f32[256,64]{0,1:T(8,128)})) %all-reduce.6.cloned.1.call-update) | async-done | bytes 131088 | tf_op jit(solution)/shard_map/psum | solution.py:57
  299.4 1.5 copy.42
  300.8 1.5 copy.43
  (3 shorter events, 0.0 us)
Async XLA Ops:
  7.2 93.1 %copy-start = (bf16[1,512,256]{2,1,0:T(8,128)(2,1)S(1)}, bf16[1,512,256]{2,1,0:T(8,128)(2,1)}, u32[]{:S(2)}) copy-start(bf16[1,512,256]{2,1,0:T(8,128)(2,1)} %param.17) | copy-start | bytes 786436
  7.2 9.5 %copy-start.1 = (bf16[1,64,16384]{2,1,0:T(8,128)(2,1)S(1)}, bf16[1,64,16384]{2,1,0:T(8,128)(2,1)}, u32[]{:S(2)}) copy-start(bf16[1,64,16384]{2,1,0:T(8,128)(2,1)} %param.9) | copy-start | bytes 6291460
  7.2 93.1 %reduce-scatter.2.cloned.1.call-start = ((), (), s32[]{:S(2)}) async-start(), calls=%async_computation.1 | async-start | bytes 4718592 | tf_op jit(solution)/shard_map/reduce_scatter | solution.py:36
  21.7 13.8 %copy-start.4 = (bf16[256,64]{0,1:T(8,128)(2,1)S(1)}, bf16[256,64]{0,1:T(8,128)(2,1)}, u32[]{:S(2)}) copy-start(bf16[256,64]{0,1:T(8,128)(2,1)} %param.15) | copy-start | bytes 98308
  35.5 2.2 copy-start.2
  37.7 5.7 %copy-start.5 = (bf16[256,64]{0,1:T(8,128)(2,1)S(1)}, bf16[256,64]{0,1:T(8,128)(2,1)}, u32[]{:S(2)}) copy-start(bf16[256,64]{0,1:T(8,128)(2,1)} %param.14) | copy-start | bytes 98308
  46.1 54.2 %copy-start.7 = (bf16[256,256]{1,0:T(8,128)(2,1)S(1)}, bf16[256,256]{1,0:T(8,128)(2,1)}, u32[]{:S(2)}) copy-start(bf16[256,256]{1,0:T(8,128)(2,1)} %param.16) | copy-start | bytes 393220
  46.1 84.7 %all-gather.2.cloned.1.call-start = ((), (), s32[]{:S(2)}) async-start(), calls=%async_computation.3 | async-start | bytes 2359296 | tf_op jit(solution)/shard_map/all_gather | solution.py:52
  102.4 160.5 %all-reduce.4.cloned.1.call-start = ((), (), s32[]{:S(2)}) async-start(), calls=%async_computation.2 | async-start | bytes 524288 | tf_op jit(solution)/shard_map/psum | solution.py:48
  104.5 32.5 %copy-start.6 = (f32[512,256]{1,0:T(8,128)S(1)}, f32[512,256]{1,0:T(8,128)}, u32[]{:S(2)}) copy-start(f32[512,256]{1,0:T(8,128)} %reduce-scatter.2.cloned.1.call-done) | copy-start | bytes 1572868
  104.5 194.9 %all-reduce.6.cloned.1.call-start = ((), (), s32[]{:S(2)}) async-start(), calls=%async_computation.4 | async-start | bytes 262144 | tf_op jit(solution)/shard_map/psum | solution.py:57
  130.8 4.9 %copy-start.3 = (bf16[4096,256]{1,0:T(8,128)(2,1)S(1)}, bf16[4096,256]{1,0:T(8,128)(2,1)}, u32[]{:S(2)}) copy-start(bf16[4096,256]{1,0:T(8,128)(2,1)} %all-gather.2.cloned.1.call-done) | copy-start | bytes 6291460
Sparse Core Ops, SparseCore 0:
  46.2 53.9 reduce-scatter.1
  102.9 27.8 all-gather.1
  137.8 124.9 all-reduce.3
  265.8 33.5 all-reduce.5
where the time goes:
time: 309 us
  waiting for transfers between devices  240 us (78%)
  local copies, waits for them, and re-layouts  30 us (10%)
  matrix products  21 us (7%)
  between operations  13.9 us (4%)
  other arithmetic  3.71 us (1%)
    psum x1, waiting for transfers between devices, body(): grad_head = lax.psum(head_local, ('feat', 'node'))  125 us
    reduce_scatter x1, waiting for transfers between devices, body(): lax.psum_scatter(contract_first(agg_part, w_neigh) + contract_first(own_p...  54.1 us
    psum x1, waiting for transfers between devices, body(): grad_neigh, grad_self = lax.psum((neigh_local, self_local), 'node')  34.7 us
    all_gather x1, waiting for transfers between devices, body(): shard_piece = lax.all_gather(grad_pre, 'feat', axis=0, tiled=True)  26.3 us
    gather x1, local copies, waits for them, and re-layouts, body(): own = jnp.take(feature_rows, target_ids[0], axis=1)  13.8 us
    unnamed x22, local copies, waits for them, and re-layouts  11.6 us
    dot_general x4, matrix products, contract_first(): lax.dot_general(left, right, (((0,), (1,)), ((), ())), preferred_element_...  10.2 us
  transfers between devices with their start and end apart: 4, of which 4 were waited for; matrix products, arithmetic and copies ran while one was open for 4% of the time, Pallas kernels for 0%

commit v1 on v0

--- a/solution.py
+++ b/solution.py
@@ -2,6 +2,27 @@
 import jax.numpy as jnp
 from jax import lax
 from jax.sharding import PartitionSpec as P
+
+
+def ring_gather(value, axis, dim):
+    length, place, rows = (lax.axis_size(axis), lax.axis_index(axis), value.shape[dim])
+    right = [(i, (i + 1) % length) for i in range(length)]
+    behind = [(i, (i - 1) % length) for i in range(length)]
+    out = jnp.zeros((*value.shape[:dim], length * rows, *value.shape[dim + 1 :]), value.dtype)
+    out = lax.dynamic_update_slice_in_dim(out, value, place * rows, axis=dim)
+    from_left = from_right = value
+    middle = length // 2
+    for turn in range(1, middle + 1):
+        from_left = lax.ppermute(from_left, axis, right)
+        out = lax.dynamic_update_slice_in_dim(
+            out, from_left, (place - turn) % length * rows, axis=dim
+        )
+        if turn < length - middle:
+            from_right = lax.ppermute(from_right, axis, behind)
+            out = lax.dynamic_update_slice_in_dim(
+                out, from_right, (place + turn) % length * rows, axis=dim
+            )
+    return out
 
 
 def aggregate_local(feature_rows, block_row, count_row, adjacency_group):
@@ -49,7 +70,7 @@
     grad_hidden = jnp.dot(cotangent, w_head, preferred_element_type=jnp.float32)
     sigma = jax.nn.sigmoid(preact)
     grad_pre = (grad_hidden * sigma * (1.0 + preact * (1.0 - sigma))).astype(jnp.bfloat16)
-    shard_piece = lax.all_gather(grad_pre, "feat", axis=0, tiled=True)
+    shard_piece = ring_gather(grad_pre, "feat", 0)
     agg_part = aggregate
     own_part = own
     neigh_local = contract_first(shard_piece, agg_part)

time: 309 us -> 289 us (0.935)
  waiting for transfers between devices: 240 us -> 210 us
  starting transfers between devices: 0.16 us -> 8.11 us
  local copies, waits for them, and re-layouts: 30 us -> 35.9 us
  matrix products: 21 us -> 16.7 us
    all_gather x1 -> x0, waiting for transfers between devices: 26.3 us -> none  [body(): shard_piece = lax.all_gather(grad_pre, 'feat', axis=0, tiled=True)]
    psum x1, waiting for transfers between devices: 125 us -> 99.9 us  [body(): grad_head = lax.psum(head_local, ('feat', 'node'))]
    ppermute x0 -> x7, waiting for transfers between devices: none -> 20.9 us  [the longest x4 20.9 us: ring_gather(): from_left = lax.ppermute(from_left, axis, right)]
    ppermute x0 -> x7, starting transfers between devices: none -> 7.99 us  [the longest x3 7.98 us: ring_gather(): from_right = lax.ppermute(from_right, axis, behind)]
    dynamic_update_slice x0 -> x7, local copies, waits for them, and re-layouts: none -> 3.96 us  [the longest x4 1.99 us: ring_gather(): lax.dynamic_update_slice_in_dim(out, from_left, (place - turn) % length *...]
    dot_general x4, matrix products: 10.2 us -> 6.99 us  [contract_first(): lax.dot_general(left, right, (((0,), (1,)), ((), ())), preferred_element_...]
    unnamed x22 -> x26, local copies, waits for them, and re-layouts: 11.6 us -> 13.4 us
  transfers between devices with their start and end apart: 4 -> 10, of which waited for: 4 -> 7; matrix products, arithmetic and copies ran while one was open for 4% -> 4% of each run, Pallas kernels for 0% -> 0%
where the time goes in v1:
time: 289 us; the launch traced here: 288 us
  waiting for transfers between devices  210 us (73%)
  local copies, waits for them, and re-layouts  35.9 us (12%)
  matrix products  16.7 us (6%)
  between operations  14 us (5%)
  starting transfers between devices  8.11 us (3%)
  other arithmetic  3.59 us (1%)
    psum x1, waiting for transfers between devices, body(): grad_head = lax.psum(head_local, ('feat', 'node'))  99.9 us
    reduce_scatter x1, waiting for transfers between devices, body(): lax.psum_scatter(contract_first(agg_part, w_neigh) + contract_first(own_p...  54.1 us
    psum x1, waiting for transfers between devices, body(): grad_neigh, grad_self = lax.psum((neigh_local, self_local), 'node')  34.9 us
    ppermute x4, waiting for transfers between devices, ring_gather(): from_left = lax.ppermute(from_left, axis, right)  20.9 us
    gather x1, local copies, waits for them, and re-layouts, body(): own = jnp.take(feature_rows, target_ids[0], axis=1)  13.8 us
    unnamed x26, local copies, waits for them, and re-layouts  13.4 us
    ppermute x3, starting transfers between devices, ring_gather(): from_right = lax.ppermute(from_right, axis, behind)  7.98 us
    dot_general x4, matrix products, contract_first(): lax.dot_general(left, right, (((0,), (1,)), ((), ())), preferred_element_...  6.99 us
  transfers between devices with their start and end apart: 10, of which 7 were waited for; matrix products, arithmetic and copies ran while one was open for 4% of the time, Pallas kernels for 0%

profile of v1, /device:TPU:0, one launch (start us, length us, event | category | flops | bytes accessed | tf_op | source)
XLA Modules:
  0.0 288.0 jit_solution(17288149852076742208)
XLA Ops:
  7.2 0.0 copy-start
  7.2 0.0 reduce-scatter.2.cloned.1.call-start
  7.2 0.7 compare_and_fusion.1
  8.0 0.8 copy.23
  8.7 0.7 bitcast_convert_fusion
  9.4 0.1 copy.22
  9.5 0.7 compare_select_fusion
  10.2 0.7 compare_and_fusion
  10.9 0.7 fusion.33
  11.7 0.1 reshape_squeeze.10
  11.8 0.0 copy-start.1
  11.8 4.9 %copy.26 = bf16[1,64,16384]{1,2,0:T(8,128)(2,1)} copy(bf16[1,64,16384]{2,1,0:T(8,128)(2,1)} %param.9) | data formatting | bytes 4194304 | tf_op args[0]
  16.7 0.0 copy-done.1
  16.7 0.6 copy.30
  17.3 1.4 copy.24
  18.7 3.1 %gather_fusion = bf16[256,64,128]{2,1,0:T(8,128)(2,1)} fusion(bf16[64,128,128]{2,0,1:T(8,128)(2,1)S(1)} %copy.24, s32[1024]{0:T(1024)S(1)} %pad_clamp_fusion), kind=kCustom, calls=%fused_computation | custom fusion | bytes 8389632 | tf_op jit(solution)/shard_map/jit(_take)/gather | solution.py:33
  21.8 13.8 %gather_fusion.1 = bf16[4096,64]{1,0:T(8,128)(2,1)S(1)} fusion(bf16[64,16384]{0,1:T(8,128)(2,1)} %bitcast.59, s32[4096]{0:T(1024)S(1)} %broadcast_clamp_fusion), kind=kCustom, calls=%fused_computation.1 | custom fusion | bytes 1064960 | tf_op jit(solution)/shard_map/jit(_take)/gather | solution.py:54
  35.5 0.0 copy-done.5
  35.6 1.5 fusion.29
  37.0 0.7 copy-done.2
  37.7 5.6 %fusion.19 = bf16[32,8,8,128]{3,2,1,0:T(8,128)(2,1)S(1)} fusion(bf16[1,32,8,128,128]{4,3,2,1,0:T(8,128)(2,1)} %param.13, bf16[64,32,8,128]{3,0,2,1:T(8,128)(2,1)S(1)} %bitcast.62, pred[32,8]{1,0:T(8,128)(4,1)S(1)} %copy.22, bf16[32,8]{1,0:T(8,128)(2,1)S(1)} %fusion.33, f32[32]{0:T(128)S(1)} %bitcast_convert_fusion), kind=kOutput, calls=%fused_computation.19 | convolution fusion | flops 541589504 | bytes 13108096 | tf_op jit(solution)/shard_map/tkrs,ftks->ftr/dot_general | solution.py:36
  43.4 0.0 copy-start.3
  43.4 0.8 copy-done.3
  44.2 2.7 convolution_add_fusion
  46.9 0.0 reduce-scatter.2.cloned.1.call-update
  46.9 0.0 copy-start.9
  46.9 0.0 all-reduce.4.cloned.1.call-start
  46.9 54.1 %reduce-scatter.2.cloned.1.call-done = f32[512,256]{1,0:T(8,128)} async-done(((f32[4096,256]{1,0:T(8,128)}), f32[512,256]{1,0:T(8,128)}) %reduce-scatter.2.cloned.1.call-update) | async-done | bytes 524304 | tf_op jit(solution)/shard_map/reduce_scatter | solution.py:57
  101.0 0.1 broadcast_in_dim.34
  101.2 0.0 copy-done
  101.2 0.0 copy-done.9
  101.2 0.9 copy-done.7
  102.1 1.0 constant_dynamic-update-slice_fusion.7
  103.1 0.0 collective-permute-start
  103.1 2.6 collective-permute-start.1
  105.7 6.4 %collective-permute-done = bf16[512,256]{1,0:T(8,128)(2,1)} collective-permute-done((bf16[512,256]{1,0:T(8,128)(2,1)}, bf16[512,256]{1,0:T(8,128)(2,1)}, u32[]{:S(2)}, u32[]{:S(2)}) %collective-permute-start) | collective-permute-done | bytes 262176 | tf_op jit(solution)/shard_map/ppermute | solution.py:16
  112.1 0.0 collective-permute-start.2
  112.1 0.0 collective-permute-done.1
  112.1 2.6 collective-permute-start.3
  114.7 2.1 convolution_bitcast_fusion
  116.8 0.0 all-reduce.4.cloned.1.call-update
  116.8 0.0 all-reduce.6.cloned.1.call-start
  116.9 4.8 %collective-permute-done.2 = bf16[512,256]{1,0:T(8,128)(2,1)} collective-permute-done((bf16[512,256]{1,0:T(8,128)(2,1)}, bf16[512,256]{1,0:T(8,128)(2,1)}, u32[]{:S(2)}, u32[]{:S(2)}) %collective-permute-start.2) | collective-permute-done | bytes 262176 | tf_op jit(solution)/shard_map/ppermute | solution.py:16
  121.7 0.0 collective-permute-start.4
  121.7 1.0 constant_dynamic-update-slice_fusion.6
  122.7 1.0 constant_dynamic-update-slice_fusion.5
  123.6 0.0 collective-permute-done.3
  123.7 2.7 collective-permute-start.5
  126.3 1.0 constant_dynamic-update-slice_fusion.4
  127.3 4.0 %collective-permute-done.4 = bf16[512,256]{1,0:T(8,128)(2,1)S(1)} collective-permute-done((bf16[512,256]{1,0:T(8,128)(2,1)}, bf16[512,256]{1,0:T(8,128)(2,1)S(1)}, u32[]{:S(2)}, u32[]{:S(2)}) %collective-permute-start.4) | collective-permute-done | bytes 262176 | tf_op jit(solution)/shard_map/ppermute | solution.py:16
  131.3 0.0 collective-permute-start.6
  131.3 1.0 constant_dynamic-update-slice_fusion.3
  132.3 0.0 collective-permute-done.5
  132.3 5.7 %collective-permute-done.6 = bf16[512,256]{1,0:T(8,128)(2,1)S(1)} collective-permute-done((bf16[512,256]{1,0:T(8,128)(2,1)S(1)}, bf16[512,256]{1,0:T(8,128)(2,1)S(1)}, u32[]{:S(2)}, u32[]{:S(2)}) %collective-permute-start.6) | collective-permute-done | bytes 262176 | tf_op jit(solution)/shard_map/ppermute | solution.py:16
  138.1 1.7 fusion.30
  139.8 0.0 copy-done.4
  139.8 1.1 fusion.24
  140.9 0.0 all-reduce.6.cloned.1.call-update
  141.0 1.0 fusion.14
  142.0 99.9 %all-reduce.4.cloned.1.call-done = f32[256,256]{0,1:T(8,128)} async-done(((f32[256,256]{0,1:T(8,128)}), f32[256,256]{0,1:T(8,128)}) %all-reduce.4.cloned.1.call-update) | async-done | bytes 262160 | tf_op jit(solution)/shard_map/psum | solution.py:69
  241.9 1.8 copy.27
  243.7 34.9 %all-reduce.6.cloned.1.call-done = (f32[256,64]{0,1:T(8,128)}, f32[256,64]{0,1:T(8,128)}) async-done(((f32[256,64]{0,1:T(8,128)}, f32[256,64]{0,1:T(8,128)}), (f32[256,64]{0,1:T(8,128)}, f32[256,64]{0,1:T(8,128)})) %all-reduce.6.cloned.1.call-update) | async-done | bytes 131088 | tf_op jit(solution)/shard_map/psum | solution.py:78
  278.6 1.5 copy.50
  280.0 1.5 copy.51
  (14 shorter events, 0.1 us)
Async XLA Ops:
  7.2 94.0 %copy-start = (bf16[1,512,256]{2,1,0:T(8,128)(2,1)S(1)}, bf16[1,512,256]{2,1,0:T(8,128)(2,1)}, u32[]{:S(2)}) copy-start(bf16[1,512,256]{2,1,0:T(8,128)(2,1)} %param.17) | copy-start | bytes 786436
  7.2 93.9 %reduce-scatter.2.cloned.1.call-start = ((), (), s32[]{:S(2)}) async-start(), calls=%async_computation.1 | async-start | bytes 4718592 | tf_op jit(solution)/shard_map/reduce_scatter | solution.py:57
  11.8 5.0 %copy-start.1 = (bf16[1,64,16384]{2,1,0:T(8,128)(2,1)S(1)}, bf16[1,64,16384]{2,1,0:T(8,128)(2,1)}, u32[]{:S(2)}) copy-start(bf16[1,64,16384]{2,1,0:T(8,128)(2,1)} %param.9) | copy-start | bytes 6291460
  21.8 13.8 %copy-start.5 = (bf16[256,64]{0,1:T(8,128)(2,1)S(1)}, bf16[256,64]{0,1:T(8,128)(2,1)}, u32[]{:S(2)}) copy-start(bf16[256,64]{0,1:T(8,128)(2,1)} %param.15) | copy-start | bytes 98308
  35.5 2.2 copy-start.2
  37.7 6.4 %copy-start.6 = (bf16[256,64]{0,1:T(8,128)(2,1)S(1)}, bf16[256,64]{0,1:T(8,128)(2,1)}, u32[]{:S(2)}) copy-start(bf16[256,64]{0,1:T(8,128)(2,1)} %param.14) | copy-start | bytes 98308
  43.4 0.8 copy-start.3
  46.9 54.3 %copy-start.9 = (bf16[256,256]{1,0:T(8,128)(2,1)S(1)}, bf16[256,256]{1,0:T(8,128)(2,1)}, u32[]{:S(2)}) copy-start(bf16[256,256]{1,0:T(8,128)(2,1)} %param.16) | copy-start | bytes 393220
  46.9 195.0 %all-reduce.4.cloned.1.call-start = ((), (), s32[]{:S(2)}) async-start(), calls=%async_computation.2 | async-start | bytes 524288 | tf_op jit(solution)/shard_map/psum | solution.py:69
  101.0 1.0 copy-start.7
  103.1 9.0 %collective-permute-start = (bf16[512,256]{1,0:T(8,128)(2,1)}, bf16[512,256]{1,0:T(8,128)(2,1)}, u32[]{:S(2)}, u32[]{:S(2)}) collective-permute-start(bf16[512,256]{1,0:T(8,128)(2,1)} %get-tuple-element.19), channel_id=1, source_target_pairs={{0,4},{4,8},{8,12},{12,16},{16,20},{20,24},{24,28},{28,0},{1,5},{5... | collective-permute-start | bytes 786440 | tf_op jit(solution)/shard_map/ppermute | solution.py:16
  103.1 9.0 %collective-permute-start.1 = (bf16[512,256]{1,0:T(8,128)(2,1)}, bf16[512,256]{1,0:T(8,128)(2,1)}, u32[]{:S(2)}, u32[]{:S(2)}) collective-permute-start(bf16[512,256]{1,0:T(8,128)(2,1)} %get-tuple-element.19), channel_id=1, source_target_pairs={{0,28},{4,0},{8,4},{12,8},{16,12},{20,16},{24,20},{28,24},{1,29},{... | collective-permute-start | bytes 786440 | tf_op jit(solution)/shard_map/ppermute | solution.py:21
  112.1 9.6 %collective-permute-start.2 = (bf16[512,256]{1,0:T(8,128)(2,1)}, bf16[512,256]{1,0:T(8,128)(2,1)}, u32[]{:S(2)}, u32[]{:S(2)}) collective-permute-start(bf16[512,256]{1,0:T(8,128)(2,1)} %collective-permute-done), channel_id=1, source_target_pairs={{0,4},{4,8},{8,12},{12,16},{16,20},{20,24},{24,28},{28,0},{1,5},{5... | collective-permute-start | bytes 786440 | tf_op jit(solution)/shard_map/ppermute | solution.py:16
  112.1 11.6 %collective-permute-start.3 = (bf16[512,256]{1,0:T(8,128)(2,1)}, bf16[512,256]{1,0:T(8,128)(2,1)}, u32[]{:S(2)}, u32[]{:S(2)}) collective-permute-start(bf16[512,256]{1,0:T(8,128)(2,1)} %collective-permute-done.1), channel_id=1, source_target_pairs={{0,28},{4,0},{8,4},{12,8},{16,12},{20,16},{24,20},{28,24},{1,29},{... | collective-permute-start | bytes 786440 | tf_op jit(solution)/shard_map/ppermute | solution.py:21
  116.8 161.7 %all-reduce.6.cloned.1.call-start = ((), (), s32[]{:S(2)}) async-start(), calls=%async_computation.3 | async-start | bytes 262144 | tf_op jit(solution)/shard_map/psum | solution.py:78
  121.7 9.6 %collective-permute-start.4 = (bf16[512,256]{1,0:T(8,128)(2,1)}, bf16[512,256]{1,0:T(8,128)(2,1)S(1)}, u32[]{:S(2)}, u32[]{:S(2)}) collective-permute-start(bf16[512,256]{1,0:T(8,128)(2,1)} %collective-permute-done.2), channel_id=1, source_target_pairs={{0,4},{4,8},{8,12},{12,16},{16,20},{20,24},{24,28},{28,0},{1,5},{5... | collective-permute-start | bytes 786440 | tf_op jit(solution)/shard_map/ppermute | solution.py:16
  123.7 8.6 %collective-permute-start.5 = (bf16[512,256]{1,0:T(8,128)(2,1)}, bf16[512,256]{1,0:T(8,128)(2,1)S(1)}, u32[]{:S(2)}, u32[]{:S(2)}) collective-permute-start(bf16[512,256]{1,0:T(8,128)(2,1)} %collective-permute-done.3), channel_id=1, source_target_pairs={{0,28},{4,0},{8,4},{12,8},{16,12},{20,16},{24,20},{28,24},{1,29},{... | collective-permute-start | bytes 786440 | tf_op jit(solution)/shard_map/ppermute | solution.py:21
  131.3 6.8 %collective-permute-start.6 = (bf16[512,256]{1,0:T(8,128)(2,1)S(1)}, bf16[512,256]{1,0:T(8,128)(2,1)S(1)}, u32[]{:S(2)}, u32[]{:S(2)}) collective-permute-start(bf16[512,256]{1,0:T(8,128)(2,1)S(1)} %collective-permute-done.4), channel_id=1, source_target_pairs={{0,4},{4,8},{8,12},{12,16},{16,20},{20,24},{24,28},{28,0},{1,5},{5... | collective-permute-start | bytes 786440 | tf_op jit(solution)/shard_map/ppermute | solution.py:16
  138.1 1.7 copy-start.4
  139.8 1.1 copy-start.8
Sparse Core Ops, SparseCore 0:
  47.0 53.9 reduce-scatter.1
  117.0 124.8 all-reduce.3
  245.0 33.5 all-reduce.5
